TPU v7x, 256 devices: a whole 4x4x8 slice. The times are simulated.
256 devices in a mesh: seq: 32 (over z_lo, y, core), head: 8 (over z_hi, x).
Axes of the slice: x: 4, y: 4, z: 8 (z_hi: 2, z_lo: 4; z = z_hi * 4 + z_lo), core: 2. Of those that a mesh axis runs over, the one named last changes fastest.
Arguments:
- queries: bfloat16 [4096, 8192], P('seq', 'head'), may hold values from -30 to 30
- cache: bfloat16 [16384, 2048], P('seq', 'head'), may hold values from -30 to 30
- stretch_kv: bfloat16 [4096, 2048], P(('seq', 'head')), may hold values from -6 to 6
- stretch_pos: int32 [32], replicated, may hold values from 0 to 31, each once
Outputs:
- attended: bfloat16 [4096, 8192], P('seq', 'head')
Inputs may be any that keep to these rules, and one draw needn't show every extreme that they name: `stretch_pos`: each block position appears once.
All inputs are finite; a program needn't handle non-finite values.
Results may differ from a plain program's by a relative error of at most 0.012.
Values may be sent and summed in bfloat16 or wider, within the bound.
A program may use at most 192 MiB of HBM per device.

v0:
```python
import math

import jax
import jax.numpy as jnp
from jax import lax
from jax.sharding import PartitionSpec as P

HD = 128


def partner(value, axis, bit):
    mask = 2**bit
    pairs = [(source, source ^ mask) for source in range(lax.axis_size(axis))]
    return lax.ppermute(value, axis, pairs)


def local_partials(qrows, qpos, keyvals, kpos, kv_heads, head_dim):
    count = qrows.shape[0]
    group = qrows.shape[1] // (kv_heads * head_dim)
    query = qrows.reshape(count, kv_heads, group, head_dim)
    pairs = keyvals.reshape(keyvals.shape[0], kv_heads, 2, head_dim)
    scores = jnp.einsum(
        "rkgd,ckd->kgrc", query, pairs[:, :, 0], preferred_element_type=jnp.float32
    ) * head_dim ** (-0.5)
    scores = jnp.where(kpos[None, None, None, :] <= qpos[None, None, :, None], scores, -1e30)
    top = jnp.max(scores, -1)
    expo = jnp.exp(scores - top[..., None])
    total = jnp.sum(expo, -1)
    summed = jnp.einsum(
        "kgrc,ckd->kgrd",
        expo.astype(jnp.bfloat16),
        pairs[:, :, 1],
        preferred_element_type=jnp.float32,
    )
    heads = kv_heads * group
    return (
        summed.reshape(heads, count, head_dim),
        top.reshape(heads, count),
        total.reshape(heads, count),
    )


def per_device(queries, cache, stretch_kv, stretch_pos):
    count = lax.axis_size("seq")
    me = lax.axis_index("seq")
    qd = queries.shape[0]
    cached = cache.shape[0]
    head_dim = HD
    kv_heads = cache.shape[1] // (2 * head_dim)
    q_heads = queries.shape[1] // head_dim
    new_local = lax.all_to_all(stretch_kv, "head", split_axis=1, concat_axis=0, tiled=True)
    own_pos = stretch_pos[me] * qd + jnp.arange(qd, dtype=jnp.int32)
    half = cached // 2
    moved = partner(cache[half:], "seq", count.bit_length() - 2)
    resident = jnp.concatenate([cache[:half], moved], 0)
    keyvals = jnp.concatenate([resident, new_local], 0)
    kpos = jnp.concatenate([jnp.full((cached,), -1, jnp.int32), own_pos])
    whole_q = lax.all_gather(queries, "seq", axis=0, tiled=True)
    qtok = whole_q.shape[0]
    block = math.gcd(qtok, 512)
    rows = jnp.arange(qtok, dtype=jnp.int32)
    qpos = stretch_pos[rows // qd] * qd + rows % qd

    def one_block(args):
        qb, pb = args
        return local_partials(qb, pb, keyvals, kpos, kv_heads, head_dim)

    summed, top, total = lax.map(
        one_block, (whole_q.reshape(qtok // block, block, -1), qpos.reshape(qtok // block, block))
    )
    summed = jnp.transpose(summed, (1, 0, 2, 3)).reshape(q_heads, qtok, head_dim)
    top = jnp.transpose(top, (1, 0, 2)).reshape(q_heads, qtok)
    total = jnp.transpose(total, (1, 0, 2)).reshape(q_heads, qtok)
    summed, top, total = (
        lax.all_to_all(summed, "seq", split_axis=1, concat_axis=1, tiled=True),
        lax.all_to_all(top, "seq", split_axis=1, concat_axis=1, tiled=True),
        lax.all_to_all(total, "seq", split_axis=1, concat_axis=1, tiled=True),
    )
    summed = summed.reshape(q_heads, count, qd, head_dim)
    top = top.reshape(q_heads, count, qd)
    total = total.reshape(q_heads, count, qd)
    best = jnp.max(top, 1, keepdims=True)
    weight = jnp.exp(top - best)
    numer = jnp.sum(weight[..., None] * summed, 1)
    denom = jnp.sum(weight * total, 1)
    result = numer / denom[..., None]
    return jnp.transpose(result, (1, 0, 2)).reshape(qd, q_heads * head_dim).astype(jnp.bfloat16)


def solution(mesh):
    return jax.shard_map(
        per_device,
        mesh=mesh,
        in_specs=(P("seq", "head"), P("seq", "head"), P(("seq", "head"), None), P()),
        out_specs=P("seq", "head"),
        check_vma=False,
    )
```

profile of v0, /device:TPU:1, one launch (start us, length us, event | category | flops | bytes accessed | tf_op | source)
XLA Modules:
  0.0 613.9 jit_solution(9171535082967741692)
XLA Ops:
  6.5 0.7 all-gather.2.cloned.1.call-update
  7.3 1.0 fusion.16
  8.4 3.9 collective-permute-start
  12.3 1.5 copy.88
  13.7 8.8 %all-to-all-start = ((bf16[16,8,256]{2,0,1:T(8,128)(2,1)}), bf16[16,8,256]{2,0,1:T(8,128)(2,1)S(1)}, u32[]{:S(2)}, u32[]{:S(2)}) async-start(bf16[16,8,256]{2,0,1:T(8,128)(2,1)} %bitcast.105), calls=%async_computation | async-start | bytes 131072 | tf_op jit(solution)/shard_map/all_to_all | solution.py:51
  24.1 1.9 fusion.18
  26.0 2.1 fusion.17
  28.0 4.3 compare_select_fusion.1
  32.4 15.5 %select_multiply_fusion = s32[4096]{0:T(1024)S(1)} fusion(pred[4096]{0:T(1024)(128)(4,1)S(1)} %compare_reduce_fusion, pred[4096]{0:T(1024)(128)(4,1)S(1)} %compare_reduce_fusion.1, pred[4096]{0:T(1024)(128)(4,1)S(1)} %compare_reduce_fusion.2, pred[4096]{0:T(1024)(128)(4,1)S(1)} %compare_reduce_fusion.3, pred[4096]{0:T(1024)(128)(4,1)S(1)} %compare_reduce_fusion.4, ...), kind=kLoop, calls=%fused_computation.68 | loop fusion | flops 106496 | bytes 135268 | tf_op jit(solution)/shard_map/mul | solution.py:62
  48.8 34.1 %all-gather.2.cloned.1.call-done = bf16[4096,1024]{1,0:T(8,128)(2,1)} async-done(((bf16[128,1024]{1,0:T(8,128)(2,1)}), bf16[4096,1024]{1,0:T(8,128)(2,1)}) %all-gather.2.cloned.1.call-update) | async-done | bytes 8388624 | tf_op jit(solution)/shard_map/all_gather | solution.py:58
  82.8 98.2 %while.14 = (s32[]{:T(128)}, f32[8,8,512,128]{3,2,0,1:T(8,128)}, f32[8,8,512]{2,1,0:T(8,128)S(1)}, f32[8,8,512]{2,1,0:T(8,128)}, s32[640]{0:T(1024)S(1)}, /*inde...) while((s32[]{:T(128)}, f32[8,8,512,128]{3,2,0,1:T(8,128)}, ...), condition=%wide.region_3.4_spmd, body=%wide.region_0.3_spmd.sunk | while | flops 1371332608 | bytes 40576612 | solution.py:68
  83.1 1.3 constant_dynamic-slice_fusion.5
  84.4 0.5 copy.90
  84.9 2.6 fusion.26
  87.5 2.8 fusion.27
  90.3 0.6 bitcast_dynamic-update-slice_fusion.6
  90.9 4.2 bitcast_dynamic-update-slice_fusion.5
  95.4 1.3 constant_dynamic-slice_fusion.5
  96.7 0.5 copy.90
  97.2 2.6 fusion.26
  99.8 2.8 fusion.27
  102.6 0.6 bitcast_dynamic-update-slice_fusion.6
  103.2 4.2 bitcast_dynamic-update-slice_fusion.5
  107.6 1.3 constant_dynamic-slice_fusion.5
  108.9 0.5 copy.90
  109.5 2.6 fusion.26
  112.1 2.8 fusion.27
  114.9 0.6 bitcast_dynamic-update-slice_fusion.6
  115.5 4.2 bitcast_dynamic-update-slice_fusion.5
  119.9 1.3 constant_dynamic-slice_fusion.5
  121.2 0.5 copy.90
  121.8 2.6 fusion.26
  124.4 2.8 fusion.27
  127.1 0.6 bitcast_dynamic-update-slice_fusion.6
  127.8 4.2 bitcast_dynamic-update-slice_fusion.5
  132.2 1.3 constant_dynamic-slice_fusion.5
  134.1 2.6 fusion.26
  136.6 2.8 fusion.27
  139.4 0.6 bitcast_dynamic-update-slice_fusion.6
  140.0 4.2 bitcast_dynamic-update-slice_fusion.5
  144.5 1.3 constant_dynamic-slice_fusion.5
  145.8 0.5 copy.90
  146.3 2.6 fusion.26
  148.9 2.8 fusion.27
  151.7 0.6 bitcast_dynamic-update-slice_fusion.6
  152.3 4.2 bitcast_dynamic-update-slice_fusion.5
  156.8 1.3 constant_dynamic-slice_fusion.5
  158.1 0.5 copy.90
  158.6 2.6 fusion.26
  161.2 2.8 fusion.27
  164.0 0.6 bitcast_dynamic-update-slice_fusion.6
  164.6 4.2 bitcast_dynamic-update-slice_fusion.5
  169.0 1.3 constant_dynamic-slice_fusion.5
  170.9 2.6 fusion.26
  173.5 2.8 fusion.27
  176.3 0.6 bitcast_dynamic-update-slice_fusion.6
  176.9 4.2 bitcast_dynamic-update-slice_fusion.5
  181.0 13.7 %all_to_all.42 = f32[8,32,128]{2,0,1:T(8,128)S(1)} all-to-all(f32[8,32,128]{2,0,1:T(8,128)S(1)} %bitcast.137), channel_id=1, replica_groups=mesh['seq'=32,'head'=8] {'seq'}, dimensions={1} | all-to-all | bytes 262144 | tf_op jit(solution)/shard_map/all_to_all | solution.py:76
  194.8 3.9 all-to-all-start.3
  198.7 17.7 %copy.65 = f32[8,4096,128]{2,0,1:T(8,128)} copy(f32[8,4096,128]{2,1,0:T(8,128)} %bitcast.54) | data formatting | bytes 33554432 | tf_op jit(solution)/shard_map/reshape | solution.py:71
  216.4 7.9 %all-to-all-start.2 = ((f32[8,4096,128]{2,0,1:T(8,128)}), f32[8,4096,128]{2,0,1:T(8,128)}, u32[]{:S(2)}, u32[]{:S(2)}) async-start(f32[8,4096,128]{2,0,1:T(8,128)} %copy.65), calls=%async_computation.2 | async-start | bytes 33554432 | tf_op jit(solution)/shard_map/all_to_all | solution.py:75
  224.4 372.6 %all-to-all-done.2 = f32[8,4096,128]{2,0,1:T(8,128)} async-done(((f32[8,4096,128]{2,0,1:T(8,128)}), f32[8,4096,128]{2,0,1:T(8,128)}, u32[]{:S(2)}, u32[]{:S(2)}) %all-to-all-start.2) | async-done | bytes 16777248 | tf_op jit(solution)/shard_map/all_to_all | solution.py:75
  597.0 8.8 %fusion.12 = f32[8,128,128]{2,1,0:T(8,128)S(1)} fusion(f32[8,32,128,128]{3,0,2,1:T(8,128)} %bitcast.55, f32[8,32,128]{2,1,0:T(8,128)S(1)} %copy.63), kind=kLoop, calls=%fused_computation.20 | loop fusion | flops 8257536 | bytes 17432576 | tf_op jit(solution)/shard_map/reduce_sum | solution.py:84
  606.2 0.9 copy.71
  (63 shorter events, 5.5 us)
Async XLA Ops:
  6.5 76.3 %all-gather.2.cloned.1.call-start = ((), (), s32[]{:S(2)}) async-start(), calls=%async_computation.4 | async-start | bytes 8650752 | tf_op jit(solution)/shard_map/all_gather | solution.py:58
  8.4 40.4 %collective-permute-start = (bf16[256,256]{0,1:T(8,128)(2,1)S(1)}, bf16[256,256]{0,1:T(8,128)(2,1)S(1)}, u32[]{:S(2)}, u32[]{:S(2)}) collective-permute-start(bf16[256,256]{0,1:T(8,128)(2,1)S(1)} %copy.80), channel_id=1, source_target_pairs={{0,128},{8,136},{16,144},{24,152},{32,160},{40,168},{48,176},{56,1... | collective-permute-start | bytes 393224 | tf_op jit(solution)/shard_map/ppermute | solution.py:14
  13.7 34.8 %all-to-all-start = ((bf16[16,8,256]{2,0,1:T(8,128)(2,1)}), bf16[16,8,256]{2,0,1:T(8,128)(2,1)S(1)}, u32[]{:S(2)}, u32[]{:S(2)}) async-start(bf16[16,8,256]{2,0,1:T(8,128)(2,1)} %bitcast.105), calls=%async_computation | async-start | bytes 131072 | tf_op jit(solution)/shard_map/all_to_all | solution.py:51
  194.8 21.6 %all-to-all-start.3 = ((f32[8,32,128]{2,0,1:T(8,128)}), f32[8,32,128]{2,0,1:T(8,128)S(1)}, u32[]{:S(2)}, u32[]{:S(2)}) async-start(f32[8,32,128]{2,0,1:T(8,128)} %bitcast.58), calls=%async_computation.3 | async-start | bytes 262144 | tf_op jit(solution)/shard_map/all_to_all | solution.py:77
  216.4 380.6 %all-to-all-start.2 = ((f32[8,4096,128]{2,0,1:T(8,128)}), f32[8,4096,128]{2,0,1:T(8,128)}, u32[]{:S(2)}, u32[]{:S(2)}) async-start(f32[8,4096,128]{2,0,1:T(8,128)} %copy.65), calls=%async_computation.2 | async-start | bytes 33554432 | tf_op jit(solution)/shard_map/all_to_all | solution.py:75
Sparse Core Ops, SparseCore 0:
  9.2 73.5 all-gather.1
where the time goes:
time: 617 us; the launch traced here: 614 us
  waiting for transfers between devices  407 us (66%)
  other arithmetic  54.7 us (9%)
  matrix products  54.1 us (9%)
  local copies, waits for them, and re-layouts  45.2 us (7%)
  starting transfers between devices  24.6 us (4%)
  between operations  14.1 us (2%)
  blocking collectives  13.7 us (2%)
    all_to_all x1, waiting for transfers between devices, per_device(): lax.all_to_all(summed, 'seq', split_axis=1, concat_axis=1, tiled=True)  373 us
    all_gather x1, waiting for transfers between devices, per_device(): whole_q = lax.all_gather(queries, 'seq', axis=0, tiled=True)  34.1 us
    dot_general x8, matrix products, local_partials(): jnp.einsum('kgrc,ckd->kgrd', expo.astype(jnp.bfloat16), pairs[:, :, 1], p...  33.4 us
    reduce_sum x8, other arithmetic, local_partials(): total = jnp.sum(expo, -1)  22.2 us
    dot_general x8, matrix products, local_partials(): jnp.einsum('rkgd,ckd->kgrc', query, pairs[:, :, 0], preferred_element_typ...  20.7 us
    reshape x1, local copies, waits for them, and re-layouts, per_device(): jnp.transpose(summed, (1, 0, 2, 3)).reshape(q_heads, qtok, head_dim)  17.7 us
    mul x1, other arithmetic, per_device(): qpos = stretch_pos[rows // qd] * qd + rows % qd  15.5 us
    dynamic_slice x24, local copies, waits for them, and re-layouts, per_device(): lax.map(one_block, (whole_q.reshape(qtok // block, block, -1), qpos.resha...  14.8 us
  transfers between devices with their start and end apart: 5, of which 2 were waited for; matrix products, arithmetic and copies ran while one was open for 7% of the time, Pallas kernels for 0%

commit v1 on v0

v1 whole, which is shorter than its diff:
```python
import functools

import jax
import jax.numpy as jnp
from jax import lax
from jax.experimental import pallas as pl
from jax.experimental.pallas import tpu as pltpu
from jax.sharding import PartitionSpec as P

MESH = pl.DeviceIdType.MESH
F32, BF16 = jnp.float32, jnp.bfloat16
HD = 128
QD = 128
CHUNK = 1024
PIECE = 512
TILE = 256
BIG = 1e30
UNITS = (
    (0, 0), (1, 0), (0, 1), (1, 1), (2, 0), (2, 1), (3, 1), (3, 0), (4, 1), (4, 0),
    (8, 1), (5, 1), (5, 0), (6, 1), (9, 1), (7, 1), (8, 0), (6, 0), (9, 0), (7, 0),
)
LAST_PARTNER = max(u for u, (_, owner) in enumerate(UNITS) if owner == 1)


def fold(x, op):
    parts = [x[8 * i : 8 * i + 8] for i in range(x.shape[0] // 8)]
    while len(parts) > 1:
        parts = [op(a, b) for a, b in zip(parts[::2], parts[1::2])]
    return parts[0]


def dot(a, b):
    return lax.dot_general(a, b, (((1,), (0,)), ((), ())), preferred_element_type=F32)


def lookup(u, values):
    found = jnp.int32(values[0])
    for k, value in enumerate(values):
        if k and value != 0:
            found = jnp.where(u == k, jnp.int32(value), found)
        elif k and values[0] != 0:
            found = jnp.where(u == k, jnp.int32(0), found)
    return found


def region(kv, slot, half, lane):
    if slot in (0, 7):
        return kv.at[slot, pl.ds(lane * 512 + half * 256, 256)]
    chunk = 2 * ((slot + 1) // 2) - 1 + half
    return kv.at[chunk, pl.ds((0 if slot % 2 else 512) + lane * 256, 256)]


def new_pair(kv, d, lane):
    return kv.at[8 + d // 2, pl.ds((d % 2) * 512 + lane * 256, 256)]


def kernel(
    q_ref, cache_ref, new_ref, pos_ref, out_ref,
    kv, vt, qt, q_in, scores, acc, top, total, tri, bias, po, plse, so, slse,
    lane_r, sib_r, yk_s, sib_s, z1_s, z3_s, all_s, all_r, loc, ny_s, ny_r, nz_r, nz1_s, nz3_s, nsib_s, nsib_r,
    q_s, q_r, o_s, o_r,
):
    me = lax.axis_index("seq")
    head = lax.axis_index("head")
    heads = 8
    core = me % 2
    y = (me // 2) % 4
    z = me // 8

    def at(zz, yy, cc):
        return {"seq": (zz * 4 + yy) * 2 + cc}

    yk = y + 1 - 2 * (y % 2)
    yp = 3 - y
    z1 = z + 1 - 2 * (z % 2)
    z2 = (z + 2) % 4
    z3 = 3 - z
    oc = 1 - core
    mid = jnp.logical_or(z == 1, z == 2)
    end = jnp.logical_or(z == 0, z == 3)
    to_sib, to_yk, to_z1, to_z3, to_p = at(z, y, oc), at(z, yk, core), at(z1, y, core), at(z3, y, core), at(z, yp, core)

    def remote(src, dst, ss, rs, dev):
        return pltpu.make_async_remote_copy(
            src_ref=src, dst_ref=dst, send_sem=ss, recv_sem=rs, device_id=dev, device_id_type=MESH
        )

    def sib(slot, h):
        src = cache_ref.at[pl.ds(h * 256, 256)] if slot == 0 else region(kv, slot, h, 0)
        return remote(src, region(kv, slot, h, 1), sib_s.at[slot, h], sib_r.at[slot, h], to_sib)

    def ykm(d, h):
        src = cache_ref.at[pl.ds(h * 256, 256)] if d == 0 else region(kv, 2 * d, h, 0)
        return remote(src, region(kv, 2 * d + 1, h, 0), yk_s.at[d, h], lane_r.at[2 * d + 1, h], to_yk)

    def z1m(d, h):
        src = cache_ref.at[pl.ds(h * 256, 256)] if d == 1 else region(kv, 6 if d == 2 else 4, h, 0)
        return remote(src, region(kv, 2 * d, h, 0), z1_s.at[d, h], lane_r.at[2 * d, h], to_z1)

    def z3m(d, h):
        src = cache_ref.at[pl.ds(h * 256, 256)] if d == 3 else region(kv, 2, h, 0)
        return remote(src, region(kv, 2 * d, h, 0), z3_s.at[d, h], lane_r.at[2 * d, h], to_z3)

    def spread(k):
        g = (head + k) % heads
        return remote(
            new_ref.at[:, pl.ds(pl.multiple_of(g * 256, 256), 256)],
            kv.at[8, pl.ds(pl.multiple_of(head * 16, 16), 16)],
            all_s.at[k], all_r.at[k], {"head": g},
        )

    def spread_in(k):
        g = (head + heads - k) % heads
        spot = kv.at[8, pl.ds(pl.multiple_of(g * 16, 16), 16)]
        return remote(spot, spot, all_s.at[k], all_r.at[k], {"head": g})

    def own_new():
        return pltpu.make_async_copy(
            new_ref.at[:, pl.ds(pl.multiple_of(head * 256, 256), 256)],
            kv.at[8, pl.ds(pl.multiple_of(head * 16, 16), 16)],
            loc.at[0],
        )

    def ny():
        return remote(kv.at[8, pl.ds(0, 128)], kv.at[8, pl.ds(128, 128)], ny_s.at[0], ny_r.at[0], to_yk)

    def nsib(d):
        return remote(new_pair(kv, d, 0), new_pair(kv, d, 1), nsib_s.at[d], nsib_r.at[d], to_sib)

    def nz1(d):
        return remote(new_pair(kv, (0, 0, 3, 2)[d], 0), new_pair(kv, d, 0), nz1_s.at[d], nz_r.at[d], to_z1)

    def nz3(d):
        return remote(new_pair(kv, 0 if d == 3 else 1, 0), new_pair(kv, d, 0), nz3_s.at[d], nz_r.at[d], to_z3)

    def qm(h):
        cols = pl.ds(h * 512, 512)
        return remote(q_ref.at[:, cols], q_in.at[:, cols], q_s.at[h], q_r.at[h], to_p)

    def om(t):
        return remote(so.at[t], po.at[t], o_s.at[t, 0], o_r.at[t, 0], to_p)

    def lm(t):
        return remote(slse.at[t], plse.at[t], o_s.at[t, 1], o_r.at[t, 1], to_p)

    barrier = pltpu.get_barrier_semaphore()
    peers = [to_sib, to_yk, to_z1, to_z3, to_p] + [{"head": (head + k) % heads} for k in range(1, heads)]
    for peer in peers:
        pl.semaphore_signal(barrier, inc=1, device_id=peer, device_id_type=MESH)

    kv[0, :512, :] = cache_ref[...]
    key_at = lax.broadcasted_iota(jnp.int32, (QD, TILE), 0)
    row_at = lax.broadcasted_iota(jnp.int32, (QD, TILE), 1) % QD
    tri[0] = jnp.zeros((QD, TILE), F32)
    tri[1] = jnp.where(key_at <= row_at, 0.0, -BIG)
    for owner in range(2):
        row_pos = pos_ref[me if owner == 0 else (z * 4 + yp) * 2 + core]
        for b in range(8):
            bias[owner * 8 + b] = jnp.float32(0.0)
        for b in range(16):
            d, lane, yr = b // 4, (b // 2) % 2, b % 2
            zz = (z, z1, z2, z3)[d]
            seq = (zz * 4 + (yk if yr else y)) * 2 + (oc if lane else core)
            if owner == 0 and b == 0:
                hidden = jnp.float32(0.0)
            else:
                hidden = jnp.where(pos_ref[seq] < row_pos, 0.0, BIG).astype(F32)
            bias[((1 + b // 8) * 2 + owner) * 8 + b % 8] = hidden
    acc[...] = jnp.zeros_like(acc)
    top[...] = jnp.full_like(top, -BIG)
    total[...] = jnp.zeros_like(total)

    def place_queries(ref, owner):
        for h in range(8):
            q = ref[:, h * HD : (h + 1) * HD].astype(F32) * (HD ** -0.5 * 1.4426950408889634)
            high = q.astype(BF16)
            low = (q - high.astype(F32)).astype(BF16)
            cols = pl.ds(owner * 1024 + h * HD, HD)
            qt[:HD, cols] = high.T
            qt[HD:, cols] = low.T

    place_queries(q_ref, 0)

    pl.semaphore_wait(barrier, len(peers))

    own_new().start()
    for h in range(2):
        qm(h).start()
        ykm(0, h).start()
        z1m(1, h).start()

        @pl.when(mid)
        def _():
            z3m(3, h).start()

        sib(0, h).start()
        if h == 0:
            for k in range(1, heads):
                spread(k).start()

    def from_yk(slot, h):
        ykm(slot // 2, h).wait_recv()
        sib(slot, h).start()

    def first_line(h):
        z1m(1, h).wait_recv()
        ykm(1, h).start()
        sib(2, h).start()

        @pl.when(mid)
        def _():
            z3m(2, h).start()
            z3m(3, h).wait_recv()
            z1m(2, h).start()

        from_yk(1, h)

    def second_line(h):
        z1m(2, h).wait_recv()
        ykm(2, h).start()
        sib(4, h).start()

        @pl.when(mid)
        def _():
            z1m(3, h).start()

        from_yk(3, h)

    def third_line(h):
        @pl.when(end)
        def _():
            z1m(3, h).wait_recv()

        ykm(3, h).start()
        sib(6, h).start()
        from_yk(5, h)

    def new_0():
        own_new().wait()
        for k in range(1, heads):
            spread_in(k).wait_recv()
        ny().start()

    def new_1():
        ny().wait_recv()
        nz1(1).start()

        @pl.when(mid)
        def _():
            nz3(3).start()

        nsib(0).start()

    def new_2():
        nz1(1).wait_recv()
        nsib(1).start()

        @pl.when(mid)
        def _():
            nz3(2).start()
            nz3(3).wait_recv()
            nz1(2).start()

    def new_3():
        nz1(2).wait_recv()
        nsib(2).start()

        @pl.when(mid)
        def _():
            nz1(3).start()

    def new_4():
        @pl.when(end)
        def _():
            nz1(3).wait_recv()

        nsib(3).start()

    def prepare(chunk):
        if chunk == 0:
            waits = [sib(0, 0), sib(0, 1)]
        elif chunk == 7:
            waits = [sib(7, 0), sib(7, 1)]
        elif chunk < 7:
            k, h = (chunk + 1) // 2, (chunk + 1) % 2
            waits = [sib(2 * k - 1, h), sib(2 * k, h)]
        else:
            waits = [nsib(2 * (chunk - 8)), nsib(2 * (chunk - 8) + 1)]
        for w in waits:
            w.wait_recv()
        vt[chunk] = kv[chunk, :, HD:].T

    def partner_queries():
        qm(0).wait_recv()
        qm(1).wait_recv()
        place_queries(q_in, 1)

    def hand_back(t):
        cols = pl.ds((4 + t) * TILE, TILE)
        weight = jnp.sum(total[:, cols], 0, keepdims=True)
        so[t] = (acc[:, cols] / weight).astype(BF16)
        slse[t] = jnp.broadcast_to(top[:1, cols] + jnp.log2(weight), (8, TILE))
        om(t).start()
        lm(t).start()

    early = {
        1: [lambda: first_line(0), new_0],
        3: [new_1],
        5: [lambda: first_line(1)],
        6: [new_2],
        10: [lambda: second_line(0)],
        12: [new_3],
        13: [lambda: second_line(1)],
        17: [new_4],
        18: [lambda: third_line(0)],
        23: [lambda: third_line(1)],
        26: [lambda: from_yk(7, 0)],
        29: [lambda: from_yk(7, 1)],
        2 * LAST_PARTNER + 1: [lambda: hand_back(0), lambda: hand_back(1)],
        2 * LAST_PARTNER + 2: [lambda: hand_back(2), lambda: hand_back(3)],
    }
    late = {}
    seen, seen_owner = {0}, {0}
    for u, (chunk, owner) in enumerate(UNITS):
        todo = []
        if chunk not in seen:
            todo.append(functools.partial(prepare, chunk))
            seen.add(chunk)
        if owner not in seen_owner:
            todo.append(partner_queries)
            seen_owner.add(owner)
        if todo:
            late[2 * u - 1] = todo

    def perform(i, table):
        for k in sorted(table):
            @pl.when(i == k)
            def _():
                for action in table[k]:
                    action()

    def bias_of(chunk, tile, b):
        return bias[(jnp.maximum(chunk - 7, 0) * 2 + tile // 4) * 8 + b]

    def piece_scores(chunk, tile, buf, j):
        k = kv[chunk, pl.ds(j * PIECE, PIECE), :HD]
        cols = pl.ds(pl.multiple_of(tile * TILE, TILE), TILE)
        s = dot(jnp.concatenate([k, k], 1), qt[:, cols])
        best = None
        for b in range(PIECE // QD):
            part = s[b * QD : (b + 1) * QD]
            if j == 0 and b == 0:
                diagonal = jnp.where(jnp.logical_and(chunk == 8, tile < 4), 1, 0)
                part = part + tri[diagonal]
            scores[buf, pl.ds(j * PIECE + b * QD, QD), :] = part
            here = fold(part, jnp.maximum) - bias_of(chunk, tile, j * (PIECE // QD) + b)
            best = here if best is None else jnp.maximum(best, here)
        return best

    def step(chunk, tile, buf, chunk2, tile2):
        cols = pl.ds(pl.multiple_of(tile * TILE, TILE), TILE)
        old = top[:, cols]
        new = jnp.maximum(old, jnp.max(scores[buf, CHUNK:, :], 0, keepdims=True))
        shrink = jnp.exp2(old - new)
        top[:, cols] = new
        best = weight = value = None
        for j in range(CHUNK // PIECE):
            here = piece_scores(chunk2, tile2, 1 - buf, j)
            best = here if best is None else jnp.maximum(best, here)
            probs = []
            for b in range(PIECE // QD):
                shift = new + bias_of(chunk, tile, j * (PIECE // QD) + b)
                s = scores[buf, pl.ds(j * PIECE + b * QD, QD), :]
                p = jnp.exp2(s.reshape(QD // 8, 8, TILE) - shift[None]).reshape(QD, TILE)
                part = fold(p, jnp.add)
                weight = part if weight is None else weight + part
                probs.append(p.astype(BF16))
            part = dot(vt[chunk, :, pl.ds(j * PIECE, PIECE)], jnp.concatenate(probs, 0))
            value = part if value is None else value + part
        scores[1 - buf, CHUNK:, :] = best
        total[:, cols] = total[:, cols] * shrink + weight
        acc[:, cols] = acc[:, cols] * shrink[:1] + value

    chunks = [c for c, _ in UNITS] + [UNITS[-1][0]]
    owners = [o for _, o in UNITS] + [UNITS[-1][1]]

    prepare(0)
    first = None
    for j in range(CHUNK // PIECE):
        here = piece_scores(jnp.int32(0), jnp.int32(0), 0, j)
        first = here if first is None else jnp.maximum(first, here)
    scores[0, CHUNK:, :] = first

    def body(i, carry):
        u, second = i // 2, i % 2
        chunk, owner = lookup(u, chunks), lookup(u, owners)
        chunk2, owner2 = lookup(u + 1, chunks), lookup(u + 1, owners)
        tile = owner * 4 + second * 2
        perform(i, early)
        step(chunk, tile, 0, chunk, tile + 1)
        perform(i, late)
        chunk_n = jnp.where(second == 1, chunk2, chunk)
        tile_n = jnp.where(second == 1, owner2 * 4, tile + 2)
        step(chunk, tile + 1, 1, chunk_n, tile_n)
        return carry

    lax.fori_loop(0, 2 * len(UNITS), body, 0)

    for t in range(4):
        om(t).wait_recv()
        lm(t).wait_recv()
        cols = pl.ds(t * TILE, TILE)
        weight = jnp.sum(total[:, cols], 0, keepdims=True)
        mine = top[:1, cols] + jnp.log2(weight)
        theirs = plse[t][:1]
        best = jnp.maximum(mine, theirs)
        a, b = jnp.exp2(mine - best), jnp.exp2(theirs - best)
        norm = 1.0 / (a + b)
        result = acc[:, cols] * (a * norm / weight) + po[t].astype(F32) * (b * norm)
        for h in range(2):
            out_ref[:, pl.ds((2 * t + h) * HD, HD)] = result[:, h * HD : (h + 1) * HD].T.astype(BF16)

    for h in range(2):
        qm(h).wait_send()
        for slot in range(8):
            sib(slot, h).wait_send()
        for d in range(4):
            ykm(d, h).wait_send()
        z1m(1, h).wait_send()

        @pl.when(mid)
        def _():
            z1m(2, h).wait_send()
            z1m(3, h).wait_send()
            z3m(2, h).wait_send()
            z3m(3, h).wait_send()

    for k in range(1, heads):
        spread(k).wait_send()
    ny().wait_send()
    nz1(1).wait_send()
    for d in range(4):
        nsib(d).wait_send()
        om(d).wait_send()
        lm(d).wait_send()

    @pl.when(mid)
    def _():
        nz1(2).wait_send()
        nz1(3).wait_send()
        nz3(2).wait_send()
        nz3(3).wait_send()


def per_device(queries, cache, stretch_kv, stretch_pos):
    dma = pltpu.SemaphoreType.DMA
    vmem = pl.BlockSpec(memory_space=pltpu.VMEM)
    return pl.pallas_call(
        kernel,
        out_shape=jax.ShapeDtypeStruct(queries.shape, BF16),
        in_specs=[vmem, vmem, vmem, pl.BlockSpec(memory_space=pltpu.SMEM)],
        out_specs=vmem,
        scratch_shapes=[
            pltpu.VMEM((10, CHUNK, 2 * HD), BF16),
            pltpu.VMEM((10, HD, CHUNK), BF16),
            pltpu.VMEM((2 * HD, 2048), BF16),
            pltpu.VMEM((QD, 1024), BF16),
            pltpu.VMEM((2, CHUNK + 8, TILE), F32),
            pltpu.VMEM((HD, 2048), F32),
            pltpu.VMEM((8, 2048), F32),
            pltpu.VMEM((8, 2048), F32),
            pltpu.VMEM((2, QD, TILE), F32),
            pltpu.SMEM((48,), F32),
            pltpu.VMEM((4, HD, TILE), BF16),
            pltpu.VMEM((4, 8, TILE), F32),
            pltpu.VMEM((4, HD, TILE), BF16),
            pltpu.VMEM((4, 8, TILE), F32),
            dma((8, 2)), dma((8, 2)), dma((4, 2)), dma((8, 2)), dma((4, 2)), dma((4, 2)),
            dma((8,)), dma((8,)), dma((1,)), dma((1,)), dma((1,)), dma((4,)), dma((4,)), dma((4,)), dma((4,)), dma((4,)),
            dma((2,)), dma((2,)), dma((4, 2)), dma((4, 2)),
        ],
        compiler_params=pltpu.CompilerParams(
            collective_id=0, has_side_effects=True, vmem_limit_bytes=40 * 2**20
        ),
        cost_estimate=pl.CostEstimate(flops=11 * 10**9, bytes_accessed=2**20, transcendentals=21 * 10**6),
        name="attend",
    )(queries, cache, stretch_kv, stretch_pos)


def solution(mesh):
    return jax.shard_map(
        per_device,
        mesh=mesh,
        in_specs=(P("seq", "head"), P("seq", "head"), P(("seq", "head"), None), P()),
        out_specs=P("seq", "head"),
        check_vma=False,
    )
```

time: 617 us -> 81.4 us (0.13)
  waiting for transfers between devices: 407 us -> 0 us
  Pallas kernels: 0 us -> 77.1 us
  other arithmetic: 54.7 us -> 0 us
  matrix products: 54.1 us -> 0 us
  local copies, waits for them, and re-layouts: 45.2 us -> 4.1 us
  starting transfers between devices: 24.6 us -> 0 us
  between operations: 14.1 us -> 0.01 us
  blocking collectives: 13.7 us -> 0 us
    all_to_all x3 -> x0, waiting for transfers between devices: 373 us -> none  [the longest x1 373 us: per_device(): lax.all_to_all(summed, 'seq', split_axis=1, concat_axis=1, tiled=True)]
    pallas_call x0 -> x1, Pallas kernels: none -> 77.1 us  [per_device(): pl.pallas_call(kernel, out_shape=jax.ShapeDtypeStruct(queries.shape, BF16...]
    dot_general x16 -> x0, matrix products: 54.1 us -> none  [the longest x8 33.4 us: local_partials(): jnp.einsum('kgrc,ckd->kgrd', expo.astype(jnp.bfloat16), pairs[:, :, 1], p...]
    all_gather x1 -> x0, waiting for transfers between devices: 34.1 us -> none  [per_device(): whole_q = lax.all_gather(queries, 'seq', axis=0, tiled=True)]
    reduce_sum x10 -> x0, other arithmetic: 31.1 us -> none  [the longest x8 22.2 us: local_partials(): total = jnp.sum(expo, -1)]
    all_to_all x3 -> x0, starting transfers between devices: 20.7 us -> none  [the longest x1 8.85 us: per_device(): lax.all_to_all(stretch_kv, 'head', split_axis=1, concat_axis=0, tiled=True)]
    reshape x1 -> x0, local copies, waits for them, and re-layouts: 17.7 us -> none  [per_device(): jnp.transpose(summed, (1, 0, 2, 3)).reshape(q_heads, qtok, head_dim)]
    mul x1 -> x0, other arithmetic: 15.5 us -> none  [per_device(): qpos = stretch_pos[rows // qd] * qd + rows % qd]
  transfers between devices with their start and end apart: 5 -> 0, of which waited for: 2 -> 0; matrix products, arithmetic and copies ran while one was open for 7% -> 0% of each run, Pallas kernels for 0% -> 0%
where the time goes in v1:
time: 81.4 us; the launch traced here: 81.2 us
  Pallas kernels  77.1 us (95%)
  local copies, waits for them, and re-layouts  4.1 us (5%)
    pallas_call x1, Pallas kernels, per_device(): pl.pallas_call(kernel, out_shape=jax.ShapeDtypeStruct(queries.shape, BF16...  77.1 us
    unnamed x9, local copies, waits for them, and re-layouts  4.1 us

profile of v1, /device:TPU:1, one launch (start us, length us, event | category | flops | bytes accessed | tf_op | source)
XLA Modules:
  0.0 81.2 jit_solution(4970226639276410658)
XLA Ops:
  0.0 0.0 copy-start
  0.0 0.9 %copy-done = bf16[128,1024]{1,0:T(8,128)(2,1)S(1)} copy-done((bf16[128,1024]{1,0:T(8,128)(2,1)S(1)}, bf16[128,1024]{1,0:T(8,128)(2,1)}, u32[]{:S(2)}) %copy-start) | copy-done | bytes 262168
  1.0 0.0 copy-start.1
  1.0 0.9 %copy-done.1 = bf16[512,256]{1,0:T(8,128)(2,1)S(1)} copy-done((bf16[512,256]{1,0:T(8,128)(2,1)S(1)}, bf16[512,256]{1,0:T(8,128)(2,1)}, u32[]{:S(2)}) %copy-start.1) | copy-done | bytes 262168
  1.9 0.0 copy-start.2
  1.9 0.8 %copy-done.2 = bf16[16,2048]{1,0:T(8,128)(2,1)S(1)} copy-done((bf16[16,2048]{1,0:T(8,128)(2,1)S(1)}, bf16[16,2048]{1,0:T(8,128)(2,1)}, u32[]{:S(2)}) %copy-start.2) | copy-done | bytes 65560
  2.7 0.0 copy-start.3
  2.7 0.7 copy-done.3
  3.4 77.1 %attend.1 = bf16[128,1024]{1,0:T(8,128)(2,1)S(1)} custom-call(bf16[128,1024]{1,0:T(8,128)(2,1)S(1)} %copy-done, bf16[512,256]{1,0:T(8,128)(2,1)S(1)} %copy-done.1, bf16[16,2048]{1,0:T(8,128)(2,1)S(1)} %copy-done.2, s32[32]{0:T(128)S(1)} %copy-done.3), custom_call_target="tpu_custom_call" | custom-call | flops 11000000512 | bytes 1048576 | tf_op jit(solution)/shard_map/attend/pallas_call | solution.py:458
  80.5 0.7 copy.6
Async XLA Ops:
  0.0 0.9 %copy-start = (bf16[128,1024]{1,0:T(8,128)(2,1)S(1)}, bf16[128,1024]{1,0:T(8,128)(2,1)}, u32[]{:S(2)}) copy-start(bf16[128,1024]{1,0:T(8,128)(2,1)} %q_ref.1) | copy-start | bytes 786436
  1.0 0.9 %copy-start.1 = (bf16[512,256]{1,0:T(8,128)(2,1)S(1)}, bf16[512,256]{1,0:T(8,128)(2,1)}, u32[]{:S(2)}) copy-start(bf16[512,256]{1,0:T(8,128)(2,1)} %cache_ref.1) | copy-start | bytes 786436
  1.9 0.8 %copy-start.2 = (bf16[16,2048]{1,0:T(8,128)(2,1)S(1)}, bf16[16,2048]{1,0:T(8,128)(2,1)}, u32[]{:S(2)}) copy-start(bf16[16,2048]{1,0:T(8,128)(2,1)} %new_ref.1) | copy-start | bytes 196612
  2.7 0.7 copy-start.3

commit v2 on v0

v2 whole, which is shorter than its diff:
```python
import functools

import jax
import jax.numpy as jnp
from jax import lax
from jax.experimental import pallas as pl
from jax.experimental.pallas import tpu as pltpu
from jax.sharding import PartitionSpec as P

MESH = pl.DeviceIdType.MESH
F32, BF16 = jnp.float32, jnp.bfloat16
HD = 128
QD = 128
BLOCK = 512
TILE = 256
BIG = 1e30
A, B, X, Y = range(4)
KINDS = ((A, B), (X, Y), (B, X), (A, Y))
ROWS = (0, 0, 1, 2)
UNITS = (0, 4, 2, 3, 1, 6, 8, 7, 5, 10, 11, 9, 16, 18, 19, 12, 17, 14, 15, 13)
LATE = (1, 1, 1, 0, 0, 1, 1, 1, 0, 0, 1, 0, 0, 0, 1, 0, 0, 0, 1, 0)
ARRIVALS = (
    ("r0",),
    ("X0_0", "r1", "A1_0", "M_0", "A1_1", "M_1", "X0_1", "n0"),
    ("A2_0",),
    ("X1_0",),
    ("A2_1",),
    ("X1_1", "nX0"),
    ("n1", "X2_0"),
    ("n2",),
    ("X2_1",),
    ("n3", "nX1"),
    ("A3_0", "nX2"),
    (),
    ("nX3", "A3_1"),
    (),
    ("X3_0",),
    (),
    ("X3_1",),
    (),
    (),
    (),
    (),
)


def fold(x, op):
    parts = [x[8 * i : 8 * i + 8] for i in range(x.shape[0] // 8)]
    while len(parts) > 1:
        parts = [op(a, b) for a, b in zip(parts[::2], parts[1::2])]
    return parts[0]


def dot(a, b):
    return lax.dot_general(a, b, (((1,), (0,)), ((), ())), preferred_element_type=F32)


def choose(index, values):
    found = jnp.int32(values[0])
    for k, value in enumerate(values[1:], 1):
        found = jnp.where(index == k, jnp.int32(value), found)
    return found


def kernel(
    q_ref, cache_ref, new_ref, pos_ref, out_ref,
    kv, vt, qt, q_own, q_in, scores, acc, top, total, tri, bias, po, plse, so, slse,
    loc, siba_s, siba_r, sibx_s, sibx_r, y_s, y_r, z1_s, z3_s, z_r, all_s, all_r,
    nz_s, nz_r, nsa_s, nsa_r, nsx_s, nsx_r, ny_s, ny_r, q_s, q_r, o_s, o_r, l_s, l_r, met,
):
    me = lax.axis_index("seq")
    head = lax.axis_index("head")
    heads = 8
    core = me % 2
    y = (me // 2) % 4
    z = me // 8

    def seq(zz, yy, cc):
        return (zz * 4 + yy) * 2 + cc

    def at(zz, yy, cc):
        return {"seq": seq(zz, yy, cc)}

    ys = (y + 3 + 2 * core) % 4
    yr = (y + 5 - 2 * core) % 4
    z1 = z + 1 - 2 * (z % 2)
    z2 = (z + 2) % 4
    z3 = 3 - z
    other = 1 - core
    mid = jnp.logical_or(z == 1, z == 2)
    end = jnp.logical_or(z == 0, z == 3)
    to_sib, to_ys, to_yr = at(z, y, other), at(z, ys, core), at(z, yr, core)
    to_z1, to_z3 = at(z1, y, core), at(z3, y, core)

    def remote(src, dst, ss, rs, dev):
        return pltpu.make_async_remote_copy(
            src_ref=src, dst_ref=dst, send_sem=ss, recv_sem=rs, device_id=dev, device_id_type=MESH
        )

    def half(d, kind, h):
        return kv.at[4 * d + kind, pl.ds(h * 256, 256)]

    def own(h):
        return cache_ref.at[pl.ds(h * 256, 256)]

    def sib_a(d, h):
        src = half(d, A, h) if d else own(h)
        return remote(src, half(d, B, h), siba_s.at[d, h], siba_r.at[d, h], to_sib)

    def sib_x(d, h):
        return remote(half(d, X, h), half(d, Y, h), sibx_s.at[d, h], sibx_r.at[d, h], to_sib)

    def along_y(d, h):
        src = half(d, A, h) if d else own(h)
        return remote(src, half(d, X, h), y_s.at[d, h], y_r.at[d, h], to_ys)

    def outward(d, h):
        src = own(h) if d == 1 else half(5 - d, A, h)
        return remote(src, half(d, A, h), z1_s.at[d, h], z_r.at[d, h], to_z1)

    def inward(d, h):
        src = own(h) if d == 3 else half(1, A, h)
        return remote(src, half(d, A, h), z3_s.at[d, h], z_r.at[d, h], to_z3)

    def fresh(kind, d):
        return kv.at[16 + kind, pl.ds(d * QD, QD)]

    def spread(k):
        g = (head + k) % heads
        return remote(
            new_ref.at[:, pl.ds(pl.multiple_of(g * 256, 256), 256)],
            kv.at[16, pl.ds(pl.multiple_of(head * 16, 16), 16)],
            all_s.at[k], all_r.at[k], {"head": g},
        )

    def spread_in(k):
        g = (head + heads - k) % heads
        spot = kv.at[16, pl.ds(pl.multiple_of(g * 16, 16), 16)]
        return remote(spot, spot, all_s.at[k], all_r.at[k], {"head": g})

    def own_new():
        return pltpu.make_async_copy(
            new_ref.at[:, pl.ds(pl.multiple_of(head * 256, 256), 256)],
            kv.at[16, pl.ds(pl.multiple_of(head * 16, 16), 16)],
            loc.at[0],
        )

    def own_cache():
        return pltpu.make_async_copy(cache_ref, kv.at[0], loc.at[1])

    def own_queries():
        return pltpu.make_async_copy(q_ref, q_own, loc.at[2])

    def new_z(d):
        return remote(fresh(A, 0), fresh(A, d), nz_s.at[d], nz_r.at[d], {1: to_z1, 2: at(z2, y, core), 3: to_z3}[d])

    def new_y(d):
        return remote(fresh(A, d), fresh(X, d), ny_s.at[d], ny_r.at[d], to_ys)

    def new_sib_a(d):
        return remote(fresh(A, d), fresh(B, d), nsa_s.at[d], nsa_r.at[d], to_sib)

    def new_sib_x(d):
        return remote(fresh(X, d), fresh(Y, d), nsx_s.at[d], nsx_r.at[d], to_sib)

    def queries(s, h):
        cols = pl.ds(h * 512, 512)
        return remote(q_ref.at[:, cols], q_in.at[s, :, cols], q_s.at[s, h], q_r.at[s, h], to_ys if s else to_yr)

    def partial(s, t):
        return remote(so.at[s, t], po.at[1 - s, t], o_s.at[s, t], o_r.at[1 - s, t], to_yr if s else to_ys)

    def partial_log(s, t):
        return remote(slse.at[s, t], plse.at[1 - s, t], l_s.at[s, t], l_r.at[1 - s, t], to_yr if s else to_ys)

    own_cache().start()
    own_queries().start()
    own_new().start()
    barrier = pltpu.get_barrier_semaphore()
    x = head % 4
    height = (head // 4) * 4 + z

    def ring(k):
        up = (height + 8 + k) % 8
        return {"seq": seq(up % 4, y, core), "head": (up // 4) * 4 + x}

    row = [{"head": (head // 4) * 4 + (x + k) % 4} for k in range(1, 4)]
    peers = [to_sib, to_ys, to_yr, ring(1), ring(-1), ring(2), ring(-2)] + row
    for peer in peers:
        pl.semaphore_signal(barrier, inc=1, device_id=peer, device_id_type=MESH)

    key_at = lax.broadcasted_iota(jnp.int32, (QD, TILE), 0)
    row_at = lax.broadcasted_iota(jnp.int32, (QD, TILE), 1) % QD
    tri[0] = jnp.zeros((QD, TILE), F32)
    tri[1] = jnp.where(key_at <= row_at, 0.0, -BIG)
    row_pos = [pos_ref[me], pos_ref[seq(z, ys, core)], pos_ref[seq(z, yr, core)]]
    places = {A: (y, core), B: (y, other), X: (yr, core), Y: (ys, other)}
    for b in range(8):
        bias[b] = jnp.float32(0.0)
    for kind, blocks in enumerate(KINDS):
        for b in range(8):
            yy, cc = places[blocks[b // 4]]
            key_pos = pos_ref[seq((z, z1, z2, z3)[b % 4], yy, cc)]
            hidden = jnp.where(key_pos < row_pos[ROWS[kind]], 0.0, BIG).astype(F32)
            bias[(1 + kind) * 8 + b] = jnp.float32(0.0) if kind == 0 and b == 0 else hidden
    acc[...] = jnp.zeros_like(acc)
    top[...] = jnp.full_like(top, -BIG)
    total[...] = jnp.zeros_like(total)

    pl.semaphore_wait(barrier, len(peers))
    for h in range(2):
        outward(1, h).start()
        pl.when(mid)(lambda: inward(3, h).start())
        along_y(0, h).start()
        sib_a(0, h).start()
        for s in range(2):
            queries(s, h).start()

    def greet(k):
        for d in (2, -2):
            pl.semaphore_signal(met.at[k], inc=1, device_id=ring(d), device_id_type=MESH)

    greet(0)

    def place_queries(ref, rows):
        for h in range(8):
            q = ref[:, h * HD : (h + 1) * HD].astype(F32) * (HD ** -0.5 * 1.4426950408889634)
            high = q.astype(BF16)
            low = (q - high.astype(F32)).astype(BF16)
            tile, cols = rows * 4 + h // 2, pl.ds(h % 2 * HD, HD)
            qt[tile, :HD, cols] = high.T
            qt[tile, HD:, cols] = low.T

    own_queries().wait()
    place_queries(q_own, 0)
    own_cache().wait()

    def on_a(d, h):
        outward(d, h).wait_recv() if d < 3 else pl.when(end)(lambda: outward(3, h).wait_recv())
        along_y(d, h).start()
        sib_a(d, h).start()
        if d < 3:
            pl.when(mid)(lambda: (inward(2, h) if d == 1 else outward(3, h)).start())

    def on_mid(h):
        @pl.when(mid)
        def _():
            inward(3, h).wait_recv()
            outward(2, h).start()

    def on_x(d, h):
        along_y(d, h).wait_recv()
        sib_x(d, h).start()

    def on_new(d):
        if d == 0:
            own_new().wait()
            for k in range(1, heads):
                spread_in(k).wait_recv()
            for k in range(1, 4):
                new_z(k).start()
        else:
            new_z(d).wait_recv()
        new_y(d).start()
        new_sib_a(d).start()

    def on_new_x(d):
        new_y(d).wait_recv()
        new_sib_x(d).start()

    def on_round(k):
        pl.semaphore_wait(met.at[k], 2)
        if k == 0:
            greet(1)
        else:
            for g in range(1, heads):
                spread(g).start()

    def arrival(name):
        if name[0] == "A":
            on_a(int(name[1]), int(name[3]))
        elif name[0] == "M":
            on_mid(int(name[2]))
        elif name[0] == "X":
            on_x(int(name[1]), int(name[3]))
        elif name[0] == "r":
            on_round(int(name[1]))
        elif name[1] == "X":
            on_new_x(int(name[2]))
        else:
            on_new(int(name[1]))

    def prepare(block):
        d, kind = block // 4, block % 4
        if d < 4:
            waits = [] if kind in (A, X) else [(sib_a if kind == B else sib_x)(d, h) for h in range(2)]
        else:
            waits = [] if kind in (A, X) else [(new_sib_a if kind == B else new_sib_x)(k) for k in range(4)]
        for w in waits:
            w.wait_recv()
        vt[block] = kv[block, :, HD:].T

    def neighbour_queries():
        for s in range(2):
            for h in range(2):
                queries(s, h).wait_recv()
            place_queries(q_in.at[s], 1 + s)

    def hand_back(s):
        for t in range(4):
            tile = 4 * (1 + s) + t
            weight = jnp.sum(total[tile], 0, keepdims=True)
            so[s, t] = (acc[tile] / weight).astype(BF16)
            slse[s, t] = jnp.broadcast_to(top[tile][:1] + jnp.log2(weight), (8, TILE))
            partial(s, t).start()
            partial_log(s, t).start()

    def parts(unit):
        d, kind = unit // 4, unit % 4
        first = 4 * d + choose(kind, [k[0] for k in KINDS])
        second = 4 * d + choose(kind, [k[1] for k in KINDS])
        shift = jnp.where(d == 4, 1 + kind, 0) * 8
        return (first, second), choose(kind, ROWS) * 4, shift, jnp.where(unit == 16, 1, 0)

    def piece_scores(unit, t, buf, j):
        blocks, tile, shift, diagonal = unit
        k = kv[blocks[j], :, :HD]
        s = dot(jnp.concatenate([k, k], 1), qt[tile + t])
        best = None
        for b in range(BLOCK // QD):
            part = s[b * QD : (b + 1) * QD]
            if j == 0 and b == 0:
                part = part + tri[diagonal]
            scores[buf, pl.ds(j * BLOCK + b * QD, QD), :] = part
            here = fold(part, jnp.maximum) - bias[shift + j * (BLOCK // QD) + b]
            best = here if best is None else jnp.maximum(best, here)
        return best

    def step(unit, t, buf, unit2, t2):
        blocks, tile, shift, _ = unit
        tile = tile + t
        old = top[tile]
        new = jnp.maximum(old, jnp.max(scores[buf, 2 * BLOCK :, :], 0, keepdims=True))
        shrink = jnp.exp2(old - new)
        top[tile] = new
        best = weight = value = None
        for j in range(2):
            here = piece_scores(unit2, t2, 1 - buf, j)
            best = here if best is None else jnp.maximum(best, here)
            probs = []
            for b in range(BLOCK // QD):
                edge = new[:1] + bias[shift + j * (BLOCK // QD) + b]
                p = jnp.exp2(scores[buf, pl.ds(j * BLOCK + b * QD, QD), :] - edge)
                part = fold(p, jnp.add)
                weight = part if weight is None else weight + part
                probs.append(p.astype(BF16))
            part = dot(vt[blocks[j]], jnp.concatenate(probs, 0))
            value = part if value is None else value + part
        scores[1 - buf, 2 * BLOCK :, :] = best
        total[tile] = total[tile] * shrink + weight
        acc[tile] = acc[tile] * shrink[:1] + value

    def first_scores(unit):
        unit = parts(jnp.int32(unit))
        scores[0, 2 * BLOCK :, :] = jnp.maximum(piece_scores(unit, 0, 0, 0), piece_scores(unit, 0, 0, 1))

    todo = [[functools.partial(arrival, name) for name in names] for names in ARRIVALS]
    ready, asked = set(), False
    for u, unit in enumerate(UNITS):
        d, kind = unit // 4, unit % 4
        when = u if LATE[u] else u - 1
        for block in (4 * d + KINDS[kind][0], 4 * d + KINDS[kind][1]):
            if block not in ready:
                ready.add(block)
                todo[when].append(functools.partial(prepare, block))
        if ROWS[kind] and not asked:
            asked = True
            todo[when].append(neighbour_queries)
        if LATE[u]:
            todo[u].append(functools.partial(first_scores, unit))
    for s in range(2):
        last = max(u for u, unit in enumerate(UNITS) if ROWS[unit % 4] == 1 + s)
        todo[last + 1].append(functools.partial(hand_back, s))

    def body(u, carry):
        code = choose(u, UNITS)
        ahead = choose(u, [code if late else unit for unit, late, code in zip(UNITS[1:], LATE[1:], UNITS)] + [UNITS[-1]])
        for k, actions in enumerate(todo[: len(UNITS)]):
            if actions:
                @pl.when(u == k)
                def _():
                    for action in actions:
                        action()

        unit, unit2 = parts(code), parts(ahead)
        for t in range(4):
            step(unit, t, t % 2, unit if t < 3 else unit2, (t + 1) % 4)
        return carry

    lax.fori_loop(0, len(UNITS), body, 0)
    for action in todo[len(UNITS)]:
        action()

    for t in range(4):
        for s in range(2):
            partial(s, t).wait_recv()
            partial_log(s, t).wait_recv()
        weight = jnp.sum(total[t], 0, keepdims=True)
        logs = [top[t][:1] + jnp.log2(weight), plse[0, t][:1], plse[1, t][:1]]
        best = jnp.maximum(logs[0], jnp.maximum(logs[1], logs[2]))
        shares = [jnp.exp2(x - best) for x in logs]
        norm = 1.0 / (shares[0] + shares[1] + shares[2])
        result = acc[t] * (shares[0] * norm / weight)
        for s in range(2):
            result = result + po[s, t].astype(F32) * (shares[1 + s] * norm)
        for h in range(2):
            out_ref[:, pl.ds((2 * t + h) * HD, HD)] = result[:, h * HD : (h + 1) * HD].T.astype(BF16)

    for k in range(1, heads):
        spread(k).wait_send()
    for h in range(2):
        for d in range(4):
            sib_a(d, h).wait_send()
            sib_x(d, h).wait_send()
            along_y(d, h).wait_send()
        outward(1, h).wait_send()
        for s in range(2):
            queries(s, h).wait_send()
    for d in range(4):
        new_sib_a(d).wait_send()
        new_sib_x(d).wait_send()
        new_y(d).wait_send()
    for d in range(1, 4):
        new_z(d).wait_send()
    for s in range(2):
        for t in range(4):
            partial(s, t).wait_send()
            partial_log(s, t).wait_send()

    @pl.when(mid)
    def _():
        for h in range(2):
            outward(2, h).wait_send()
            outward(3, h).wait_send()
            inward(2, h).wait_send()
            inward(3, h).wait_send()


def per_device(queries, cache, stretch_kv, stretch_pos):
    dma = pltpu.SemaphoreType.DMA
    hbm = pl.BlockSpec(memory_space=pltpu.HBM)
    return pl.pallas_call(
        kernel,
        out_shape=jax.ShapeDtypeStruct(queries.shape, BF16),
        in_specs=[hbm, hbm, hbm, pl.BlockSpec(memory_space=pltpu.SMEM)],
        out_specs=pl.BlockSpec(memory_space=pltpu.VMEM),
        scratch_shapes=[
            pltpu.VMEM((20, BLOCK, 2 * HD), BF16),
            pltpu.VMEM((20, HD, BLOCK), BF16),
            pltpu.VMEM((12, 2 * HD, TILE), BF16),
            pltpu.VMEM((QD, 1024), BF16),
            pltpu.VMEM((2, QD, 1024), BF16),
            pltpu.VMEM((2, 2 * BLOCK + 8, TILE), F32),
            pltpu.VMEM((12, HD, TILE), F32),
            pltpu.VMEM((12, 8, TILE), F32),
            pltpu.VMEM((12, 8, TILE), F32),
            pltpu.VMEM((2, QD, TILE), F32),
            pltpu.SMEM((40,), F32),
            pltpu.VMEM((2, 4, HD, TILE), BF16),
            pltpu.VMEM((2, 4, 8, TILE), F32),
            pltpu.VMEM((2, 4, HD, TILE), BF16),
            pltpu.VMEM((2, 4, 8, TILE), F32),
            dma((3,)), dma((4, 2)), dma((4, 2)), dma((4, 2)), dma((4, 2)), dma((4, 2)), dma((4, 2)),
            dma((4, 2)), dma((4, 2)), dma((4, 2)), dma((8,)), dma((8,)),
            dma((4,)), dma((4,)), dma((4,)), dma((4,)), dma((4,)), dma((4,)), dma((4,)), dma((4,)),
            dma((2, 2)), dma((2, 2)), dma((2, 4)), dma((2, 4)), dma((2, 4)), dma((2, 4)),
            pltpu.SemaphoreType.REGULAR((2,)),
        ],
        compiler_params=pltpu.CompilerParams(
            collective_id=0, has_side_effects=True, vmem_limit_bytes=60 * 2**20
        ),
        cost_estimate=pl.CostEstimate(flops=11 * 10**9, bytes_accessed=2**20, transcendentals=21 * 10**6),
        name="attend",
    )(queries, cache, stretch_kv, stretch_pos)


def solution(mesh):
    return jax.shard_map(
        per_device,
        mesh=mesh,
        in_specs=(P("seq", "head"), P("seq", "head"), P(("seq", "head"), None), P()),
        out_specs=P("seq", "head"),
        check_vma=False,
    )
```

time: 617 us -> 59.9 us (0.10)
  waiting for transfers between devices: 407 us -> 0 us
  Pallas kernels: 0 us -> 58.1 us
  other arithmetic: 54.7 us -> 0 us
  matrix products: 54.1 us -> 0 us
  local copies, waits for them, and re-layouts: 45.2 us -> 1.67 us
  starting transfers between devices: 24.6 us -> 0 us
  between operations: 14.1 us -> 0.01 us
  blocking collectives: 13.7 us -> 0 us
    all_to_all x3 -> x0, waiting for transfers between devices: 373 us -> none  [the longest x1 373 us: per_device(): lax.all_to_all(summed, 'seq', split_axis=1, concat_axis=1, tiled=True)]
    pallas_call x0 -> x1, Pallas kernels: none -> 58.1 us  [per_device(): pl.pallas_call(kernel, out_shape=jax.ShapeDtypeStruct(queries.shape, BF16...]
    dot_general x16 -> x0, matrix products: 54.1 us -> none  [the longest x8 33.4 us: local_partials(): jnp.einsum('kgrc,ckd->kgrd', expo.astype(jnp.bfloat16), pairs[:, :, 1], p...]
    all_gather x1 -> x0, waiting for transfers between devices: 34.1 us -> none  [per_device(): whole_q = lax.all_gather(queries, 'seq', axis=0, tiled=True)]
    reduce_sum x10 -> x0, other arithmetic: 31.1 us -> none  [the longest x8 22.2 us: local_partials(): total = jnp.sum(expo, -1)]
    all_to_all x3 -> x0, starting transfers between devices: 20.7 us -> none  [the longest x1 8.85 us: per_device(): lax.all_to_all(stretch_kv, 'head', split_axis=1, concat_axis=0, tiled=True)]
    reshape x1 -> x0, local copies, waits for them, and re-layouts: 17.7 us -> none  [per_device(): jnp.transpose(summed, (1, 0, 2, 3)).reshape(q_heads, qtok, head_dim)]
    mul x1 -> x0, other arithmetic: 15.5 us -> none  [per_device(): qpos = stretch_pos[rows // qd] * qd + rows % qd]
  transfers between devices with their start and end apart: 5 -> 0, of which waited for: 2 -> 0; matrix products, arithmetic and copies ran while one was open for 7% -> 0% of each run, Pallas kernels for 0% -> 0%
where the time goes in v2:
time: 59.9 us; the launch traced here: 59.8 us
  Pallas kernels  58.1 us (97%)
  local copies, waits for them, and re-layouts  1.67 us (3%)
    pallas_call x1, Pallas kernels, per_device(): pl.pallas_call(kernel, out_shape=jax.ShapeDtypeStruct(queries.shape, BF16...  58.1 us
    unnamed x1, local copies, waits for them, and re-layouts  1.67 us

profile of v2, /device:TPU:1, one launch (start us, length us, event | category | flops | bytes accessed | tf_op | source)
XLA Modules:
  0.0 59.8 jit_solution(11268691571042694124)
XLA Ops:
  0.0 58.1 %attend.1 = bf16[128,1024]{1,0:T(8,128)(2,1)} custom-call(bf16[128,1024]{1,0:T(8,128)(2,1)} %q_ref.1, bf16[512,256]{1,0:T(8,128)(2,1)} %cache_ref.1, bf16[16,2048]{1,0:T(8,128)(2,1)} %new_ref.1, s32[32]{0:T(128)} %pos_ref.1), custom_call_target="tpu_custom_call" | custom-call | flops 11000000512 | bytes 1048576 | tf_op jit(solution)/shard_map/attend/pallas_call | solution.py:452
  58.1 1.7 %copy.6 = bf16[128,1024]{1,0:T(8,128)(2,1)} copy(bf16[128,1024]{1,0:T(8,128)(2,1)} %attend.1) | data formatting | bytes 524288

commit v3 on v2

--- a/solution.py
+++ b/solution.py
@@ -17,26 +17,26 @@
 A, B, X, Y = range(4)
 KINDS = ((A, B), (X, Y), (B, X), (A, Y))
 ROWS = (0, 0, 1, 2)
-UNITS = (0, 4, 2, 3, 1, 6, 8, 7, 5, 10, 11, 9, 16, 18, 19, 12, 17, 14, 15, 13)
-LATE = (1, 1, 1, 0, 0, 1, 1, 1, 0, 0, 1, 0, 0, 0, 1, 0, 0, 0, 1, 0)
+UNITS = (0, 4, 2, 3, 1, 6, 8, 7, 5, 10, 11, 14, 15, 18, 19, 9, 12, 13, 16, 17)
+LATE = (1, 1, 1, 0, 0, 0, 1, 1, 0, 0, 1, 1, 1, 1, 1, 0, 0, 0, 0, 0)
 ARRIVALS = (
     ("r0",),
-    ("X0_0", "r1", "A1_0", "M_0", "A1_1", "M_1", "X0_1", "n0"),
+    ("r1", "X0_0", "A1_0", "M_0", "r2", "r3", "A1_1", "M_1", "X0_1"),
     ("A2_0",),
     ("X1_0",),
-    ("A2_1",),
-    ("X1_1", "nX0"),
-    ("n1", "X2_0"),
-    ("n2",),
+    ("A2_1", "X1_1"),
+    (),
+    ("n0", "X2_0"),
+    ("A3_0",),
     ("X2_1",),
+    ("nX0", "A3_1"),
+    (),
+    ("n1", "X3_0", "n2", "X3_1"),
     ("n3", "nX1"),
-    ("A3_0", "nX2"),
-    (),
-    ("nX3", "A3_1"),
-    (),
-    ("X3_0",),
-    (),
-    ("X3_1",),
+    ("nX2", "nX3"),
+    (),
+    (),
+    (),
     (),
     (),
     (),
@@ -180,14 +180,24 @@
     x = head % 4
     height = (head // 4) * 4 + z
 
-    def ring(k):
+    def line(k):
         up = (height + 8 + k) % 8
         return {"seq": seq(up % 4, y, core), "head": (up // 4) * 4 + x}
 
-    row = [{"head": (head // 4) * 4 + (x + k) % 4} for k in range(1, 4)]
-    peers = [to_sib, to_ys, to_yr, ring(1), ring(-1), ring(2), ring(-2)] + row
+    def greet(sem):
+        @pl.when(height < 7)
+        def _():
+            pl.semaphore_signal(sem, inc=1, device_id=line(1), device_id_type=MESH)
+
+        @pl.when(height > 0)
+        def _():
+            pl.semaphore_signal(sem, inc=1, device_id=line(-1), device_id_type=MESH)
+
+    adjoining = jnp.where(jnp.logical_or(height == 0, height == 7), 1, 2)
+    peers = [to_sib, to_ys, to_yr] + [{"head": (head // 4) * 4 + (x + k) % 4} for k in range(1, 4)]
     for peer in peers:
         pl.semaphore_signal(barrier, inc=1, device_id=peer, device_id_type=MESH)
+    greet(barrier)
 
     key_at = lax.broadcasted_iota(jnp.int32, (QD, TILE), 0)
     row_at = lax.broadcasted_iota(jnp.int32, (QD, TILE), 1) % QD
@@ -207,7 +217,7 @@
     top[...] = jnp.full_like(top, -BIG)
     total[...] = jnp.zeros_like(total)
 
-    pl.semaphore_wait(barrier, len(peers))
+    pl.semaphore_wait(barrier, len(peers) + adjoining)
     for h in range(2):
         outward(1, h).start()
         pl.when(mid)(lambda: inward(3, h).start())
@@ -216,11 +226,7 @@
         for s in range(2):
             queries(s, h).start()
 
-    def greet(k):
-        for d in (2, -2):
-            pl.semaphore_signal(met.at[k], inc=1, device_id=ring(d), device_id_type=MESH)
-
-    greet(0)
+    greet(met.at[0])
 
     def place_queries(ref, rows):
         for h in range(8):
@@ -269,9 +275,9 @@
         new_sib_x(d).start()
 
     def on_round(k):
-        pl.semaphore_wait(met.at[k], 2)
-        if k == 0:
-            greet(1)
+        pl.semaphore_wait(met.at[k], adjoining)
+        if k < 3:
+            greet(met.at[k + 1])
         else:
             for g in range(1, heads):
                 spread(g).start()
@@ -451,7 +457,7 @@
     hbm = pl.BlockSpec(memory_space=pltpu.HBM)
     return pl.pallas_call(
         kernel,
-        out_shape=jax.ShapeDtypeStruct(queries.shape, BF16),
+        out_shape=pltpu.VMEM(queries.shape, BF16),
         in_specs=[hbm, hbm, hbm, pl.BlockSpec(memory_space=pltpu.SMEM)],
         out_specs=pl.BlockSpec(memory_space=pltpu.VMEM),
         scratch_shapes=[
@@ -474,7 +480,7 @@
             dma((4, 2)), dma((4, 2)), dma((4, 2)), dma((8,)), dma((8,)),
             dma((4,)), dma((4,)), dma((4,)), dma((4,)), dma((4,)), dma((4,)), dma((4,)), dma((4,)),
             dma((2, 2)), dma((2, 2)), dma((2, 4)), dma((2, 4)), dma((2, 4)), dma((2, 4)),
-            pltpu.SemaphoreType.REGULAR((2,)),
+            pltpu.SemaphoreType.REGULAR((4,)),
         ],
         compiler_params=pltpu.CompilerParams(
             collective_id=0, has_side_effects=True, vmem_limit_bytes=60 * 2**20

time: 59.9 us -> 52.1 us (0.87)
  Pallas kernels: 58.1 us -> 51.2 us
  local copies, waits for them, and re-layouts: 1.67 us -> 0.71 us
    pallas_call x1, Pallas kernels: 58.1 us -> 51.2 us  [per_device(): pl.pallas_call(kernel, out_shape=pltpu.VMEM(queries.shape, BF16), in_spec...]
    unnamed x1, local copies, waits for them, and re-layouts: 1.67 us -> 0.71 us
where the time goes in v3:
time: 52.1 us; the launch traced here: 51.9 us
  Pallas kernels  51.2 us (98%)
  local copies, waits for them, and re-layouts  0.71 us (1%)
    pallas_call x1, Pallas kernels, per_device(): pl.pallas_call(kernel, out_shape=pltpu.VMEM(queries.shape, BF16), in_spec...  51.2 us

profile of v3, /device:TPU:1, one launch (start us, length us, event | category | flops | bytes accessed | tf_op | source)
XLA Modules:
  0.0 51.9 jit_solution(8677050840183895535)
XLA Ops:
  0.0 51.2 %attend.1 = bf16[128,1024]{1,0:T(8,128)(2,1)S(1)} custom-call(bf16[128,1024]{1,0:T(8,128)(2,1)} %q_ref.1, bf16[512,256]{1,0:T(8,128)(2,1)} %cache_ref.1, bf16[16,2048]{1,0:T(8,128)(2,1)} %new_ref.1, s32[32]{0:T(128)} %pos_ref.1), custom_call_target="tpu_custom_call" | custom-call | flops 11000000512 | bytes 1048576 | tf_op jit(solution)/shard_map/attend/pallas_call | solution.py:458
  51.2 0.7 %copy.6 = bf16[128,1024]{1,0:T(8,128)(2,1)} copy(bf16[128,1024]{1,0:T(8,128)(2,1)S(1)} %attend.1) | data formatting | bytes 524288

commit v4 on v3

--- a/solution.py
+++ b/solution.py
@@ -160,8 +160,8 @@
     def new_sib_a(d):
         return remote(fresh(A, d), fresh(B, d), nsa_s.at[d], nsa_r.at[d], to_sib)
 
-    def new_sib_x(d):
-        return remote(fresh(X, d), fresh(Y, d), nsx_s.at[d], nsx_r.at[d], to_sib)
+    def new_y_other(d):
+        return remote(fresh(A, d), fresh(Y, d), nsx_s.at[d], nsx_r.at[d], at(z, ys, other))
 
     def queries(s, h):
         cols = pl.ds(h * 512, 512)
@@ -268,11 +268,11 @@
         else:
             new_z(d).wait_recv()
         new_y(d).start()
+        new_y_other(d).start()
         new_sib_a(d).start()
 
     def on_new_x(d):
         new_y(d).wait_recv()
-        new_sib_x(d).start()
 
     def on_round(k):
         pl.semaphore_wait(met.at[k], adjoining)
@@ -301,7 +301,7 @@
         if d < 4:
             waits = [] if kind in (A, X) else [(sib_a if kind == B else sib_x)(d, h) for h in range(2)]
         else:
-            waits = [] if kind in (A, X) else [(new_sib_a if kind == B else new_sib_x)(k) for k in range(4)]
+            waits = [] if kind in (A, X) else [(new_sib_a if kind == B else new_y_other)(k) for k in range(4)]
         for w in waits:
             w.wait_recv()
         vt[block] = kv[block, :, HD:].T
@@ -434,7 +434,7 @@
             queries(s, h).wait_send()
     for d in range(4):
         new_sib_a(d).wait_send()
-        new_sib_x(d).wait_send()
+        new_y_other(d).wait_send()
         new_y(d).wait_send()
     for d in range(1, 4):
         new_z(d).wait_send()

time: 52.1 us -> 51.6 us (level)
  Pallas kernels: 51.2 us -> 50.6 us
    pallas_call x1, Pallas kernels: 51.2 us -> 50.6 us  [per_device(): pl.pallas_call(kernel, out_shape=pltpu.VMEM(queries.shape, BF16), in_spec...]
where the time goes in v4:
time: 51.6 us; the launch traced here: 51.3 us
  Pallas kernels  50.6 us (98%)
  local copies, waits for them, and re-layouts  0.71 us (1%)
    pallas_call x1, Pallas kernels, per_device(): pl.pallas_call(kernel, out_shape=pltpu.VMEM(queries.shape, BF16), in_spec...  50.6 us

profile of v4, /device:TPU:1, one launch (start us, length us, event | category | flops | bytes accessed | tf_op | source)
XLA Modules:
  0.0 51.3 jit_solution(10233197505458143535)
XLA Ops:
  0.0 50.6 %attend.1 = bf16[128,1024]{1,0:T(8,128)(2,1)S(1)} custom-call(bf16[128,1024]{1,0:T(8,128)(2,1)} %q_ref.1, bf16[512,256]{1,0:T(8,128)(2,1)} %cache_ref.1, bf16[16,2048]{1,0:T(8,128)(2,1)} %new_ref.1, s32[32]{0:T(128)} %pos_ref.1), custom_call_target="tpu_custom_call" | custom-call | flops 11000000512 | bytes 1048576 | tf_op jit(solution)/shard_map/attend/pallas_call | solution.py:458
  50.6 0.7 %copy.6 = bf16[128,1024]{1,0:T(8,128)(2,1)} copy(bf16[128,1024]{1,0:T(8,128)(2,1)S(1)} %attend.1) | data formatting | bytes 524288

commit v5 on v4

--- a/solution.py
+++ b/solution.py
@@ -170,8 +170,8 @@
     def partial(s, t):
         return remote(so.at[s, t], po.at[1 - s, t], o_s.at[s, t], o_r.at[1 - s, t], to_yr if s else to_ys)
 
-    def partial_log(s, t):
-        return remote(slse.at[s, t], plse.at[1 - s, t], l_s.at[s, t], l_r.at[1 - s, t], to_yr if s else to_ys)
+    def partial_logs(s):
+        return remote(slse.at[s], plse.at[1 - s], l_s.at[s], l_r.at[1 - s], to_yr if s else to_ys)
 
     own_cache().start()
     own_queries().start()
@@ -313,13 +313,15 @@
             place_queries(q_in.at[s], 1 + s)
 
     def hand_back(s):
+        logs = []
         for t in range(4):
             tile = 4 * (1 + s) + t
             weight = jnp.sum(total[tile], 0, keepdims=True)
             so[s, t] = (acc[tile] / weight).astype(BF16)
-            slse[s, t] = jnp.broadcast_to(top[tile][:1] + jnp.log2(weight), (8, TILE))
+            logs.append(top[tile][:1] + jnp.log2(weight))
             partial(s, t).start()
-            partial_log(s, t).start()
+        slse[s] = jnp.concatenate(logs + logs, 0)
+        partial_logs(s).start()
 
     def parts(unit):
         d, kind = unit // 4, unit % 4
@@ -407,12 +409,13 @@
     for action in todo[len(UNITS)]:
         action()
 
+    for s in range(2):
+        partial_logs(s).wait_recv()
     for t in range(4):
         for s in range(2):
             partial(s, t).wait_recv()
-            partial_log(s, t).wait_recv()
         weight = jnp.sum(total[t], 0, keepdims=True)
-        logs = [top[t][:1] + jnp.log2(weight), plse[0, t][:1], plse[1, t][:1]]
+        logs = [top[t][:1] + jnp.log2(weight), plse[0, pl.ds(t, 1)], plse[1, pl.ds(t, 1)]]
         best = jnp.maximum(logs[0], jnp.maximum(logs[1], logs[2]))
         shares = [jnp.exp2(x - best) for x in logs]
         norm = 1.0 / (shares[0] + shares[1] + shares[2])
@@ -439,9 +442,9 @@
     for d in range(1, 4):
         new_z(d).wait_send()
     for s in range(2):
+        partial_logs(s).wait_send()
         for t in range(4):
             partial(s, t).wait_send()
-            partial_log(s, t).wait_send()
 
     @pl.when(mid)
     def _():
@@ -473,13 +476,13 @@
             pltpu.VMEM((2, QD, TILE), F32),
             pltpu.SMEM((40,), F32),
             pltpu.VMEM((2, 4, HD, TILE), BF16),
-            pltpu.VMEM((2, 4, 8, TILE), F32),
+            pltpu.VMEM((2, 8, TILE), F32),
             pltpu.VMEM((2, 4, HD, TILE), BF16),
-            pltpu.VMEM((2, 4, 8, TILE), F32),
+            pltpu.VMEM((2, 8, TILE), F32),
             dma((3,)), dma((4, 2)), dma((4, 2)), dma((4, 2)), dma((4, 2)), dma((4, 2)), dma((4, 2)),
             dma((4, 2)), dma((4, 2)), dma((4, 2)), dma((8,)), dma((8,)),
             dma((4,)), dma((4,)), dma((4,)), dma((4,)), dma((4,)), dma((4,)), dma((4,)), dma((4,)),
-            dma((2, 2)), dma((2, 2)), dma((2, 4)), dma((2, 4)), dma((2, 4)), dma((2, 4)),
+            dma((2, 2)), dma((2, 2)), dma((2, 4)), dma((2, 4)), dma((2,)), dma((2,)),
             pltpu.SemaphoreType.REGULAR((4,)),
         ],
         compiler_params=pltpu.CompilerParams(

time: 51.6 us -> 51.4 us (level)
  no operation moved by 1% of the time
where the time goes in v5:
time: 51.4 us; the launch traced here: 51.1 us
  Pallas kernels  50.4 us (98%)
  local copies, waits for them, and re-layouts  0.71 us (1%)
    pallas_call x1, Pallas kernels, per_device(): pl.pallas_call(kernel, out_shape=pltpu.VMEM(queries.shape, BF16), in_spec...  50.4 us

profile of v5, /device:TPU:1, one launch (start us, length us, event | category | flops | bytes accessed | tf_op | source)
XLA Modules:
  0.0 51.1 jit_solution(2463278662024031969)
XLA Ops:
  0.0 50.4 %attend.1 = bf16[128,1024]{1,0:T(8,128)(2,1)S(1)} custom-call(bf16[128,1024]{1,0:T(8,128)(2,1)} %q_ref.1, bf16[512,256]{1,0:T(8,128)(2,1)} %cache_ref.1, bf16[16,2048]{1,0:T(8,128)(2,1)} %new_ref.1, s32[32]{0:T(128)} %pos_ref.1), custom_call_target="tpu_custom_call" | custom-call | flops 11000000512 | bytes 1048576 | tf_op jit(solution)/shard_map/attend/pallas_call | solution.py:461
  50.4 0.7 %copy.6 = bf16[128,1024]{1,0:T(8,128)(2,1)} copy(bf16[128,1024]{1,0:T(8,128)(2,1)S(1)} %attend.1) | data formatting | bytes 524288
